TPU v7x, 128 devices: a whole 4x4x4 slice. The times are simulated.
128 devices in a mesh: wide: 16 (over x, z), narrow: 8 (over y, core).
Axes of the slice: x: 4, y: 4, z: 4, core: 2. Of those that a mesh axis runs over, the one named last changes fastest.
Arguments:
- pair_density: bfloat16 [2, 7680, 6144], P(None, ('wide', 'narrow')), may hold values from -0.21875 to 0.21875
- g_index: int32 [7680], P(('wide', 'narrow')), may hold values from 0 to 15359, as said below
- coulomb_table: float32 [15360], replicated, may hold values from 0.1 to 10
- eps_valence: float32 [300], replicated, may hold values from -20 to -4
- eps_conduction: float32 [300], replicated, may hold values from 4 to 20
- valence_band: int32 [6144], P('narrow'), may hold values from 0 to 299
- conduction_band: int32 [6144], P('narrow'), may hold values from 0 to 299
Outputs:
- hamiltonian: float32 [2, 6144, 6144], P(None, 'narrow', 'wide')
Inputs may be any that keep to these rules, and one draw needn't show every extreme that they name: `g_index`: increasing; entry i is 2 i or 2 i + 1, so all entries differ.
All inputs are finite; a program needn't handle non-finite values.
Results may differ from a plain program's by a relative error of at most 0.0045.
Values may be sent and summed in bfloat16 or wider, within the bound.
No kernel may reach another device: no remote copies, remote signals or barrier semaphores. Data moves between devices by JAX's collectives and lax.ppermute only.
A program may use at most 320 MiB of HBM per device.

v0:
```python
import jax
import jax.numpy as jnp
from jax import lax
from jax.sharding import PartitionSpec as P


def regroup(first_src, second_src):
    result = (
        lax.all_to_all(first_src, ("wide", "narrow"), split_axis=2, concat_axis=1, tiled=True),
        lax.all_to_all(second_src, ("wide", "narrow"), split_axis=2, concat_axis=1, tiled=True),
    )
    return result


def tile_pair(row_side, col_side):
    real_part = jnp.einsum("pgk,pgb->kb", row_side, col_side, preferred_element_type=jnp.float32)
    imag_first = jnp.einsum(
        "gk,gb->kb", row_side[0], col_side[1], preferred_element_type=jnp.float32
    )
    imag_second = jnp.einsum(
        "gk,gb->kb", row_side[1], col_side[0], preferred_element_type=jnp.float32
    )
    return jnp.stack([real_part, imag_first - imag_second])


def band_lookup(band_ids, table):
    levels = jnp.arange(table.shape[0], dtype=jnp.int32)
    onehot_mask = band_ids[:, None] == levels[None, :]
    return jnp.sum(jnp.where(onehot_mask, table[None, :], 0.0), axis=1)


def per_device(
    pair_density, g_index, coulomb_table, eps_valence, eps_conduction, valence_band, conduction_band
):
    wide_count = lax.axis_size("wide")
    narrow_count = lax.axis_size("narrow")
    local_g = pair_density.shape[1]
    total_trans = pair_density.shape[2]
    col_width = total_trans // wide_count
    row_width = total_trans // narrow_count
    slice_width = col_width // narrow_count
    weight = jnp.sqrt(jnp.take(coulomb_table, g_index))
    scaled = (pair_density.astype(jnp.float32) * weight[None, :, None]).astype(jnp.bfloat16)
    row_order = scaled.reshape(2, local_g, narrow_count, wide_count, slice_width)
    row_order = row_order.transpose(0, 1, 3, 2, 4).reshape(2, local_g, total_trans)
    col_part, row_part = regroup(scaled, row_order)
    col_block = lax.all_gather(col_part, "narrow", axis=2, tiled=True)
    kernel_tile = tile_pair(lax.all_gather(row_part, "wide", axis=2, tiled=True), col_block)
    narrow_pos = lax.axis_index("narrow")
    wide_pos = lax.axis_index("wide")
    row_ids = narrow_pos * row_width + jnp.arange(row_width, dtype=jnp.int32)
    col_ids = wide_pos * col_width + jnp.arange(col_width, dtype=jnp.int32)
    energy_gap = band_lookup(conduction_band, eps_conduction) - band_lookup(
        valence_band, eps_valence
    )
    diagonal = jnp.where(row_ids[:, None] == col_ids[None, :], energy_gap[:, None], 0.0)
    return jnp.stack([2.0 * kernel_tile[0] + diagonal, 2.0 * kernel_tile[1]])


def solution(mesh):
    placed = (
        P(None, ("wide", "narrow"), None),
        P(("wide", "narrow")),
        P(),
        P(),
        P(),
        P("narrow"),
        P("narrow"),
    )
    return jax.shard_map(
        per_device, mesh=mesh, in_specs=placed, out_specs=P(None, "narrow", "wide"), check_vma=False
    )
```

profile of v0, /device:TPU:1, one launch (start us, length us, event | category | flops | bytes accessed | tf_op | source)
XLA Modules:
  0.0 364.9 jit_solution(12060292012092193039)
XLA Ops:
  6.5 0.0 copy-start
  6.5 0.0 all-gather.5.cloned.1.call-start
  6.5 0.7 compare_select_fusion
  7.2 0.2 copy-done
  7.4 0.8 gather_fusion
  8.2 0.7 fusion.8
  8.8 1.9 multiply_convert_fusion
  10.8 5.3 %copy.43 = bf16[2,60,6144]{1,0,2:T(2,128)(2,1)} copy(bf16[2,60,6144]{2,1,0:T(8,128)(2,1)S(1)} %multiply_convert_fusion) | data formatting | bytes 2949120 | tf_op jit(solution)/shard_map/convert_element_type | solution.py:43
  16.1 12.4 %reshape.47 = bf16[128,2,2880]{2,1,0:T(2,128)(2,1)S(1)} reshape(bf16[6144,2,60]{2,1,0:T(2,128)(2,1)} %bitcast.70) | data formatting | bytes 2949120
  28.5 35.4 %all_to_all.36 = bf16[128,2,2880]{2,1,0:T(2,128)(2,1)} all-to-all(bf16[128,2,2880]{2,1,0:T(2,128)(2,1)S(1)} %reshape.47), channel_id=1, replica_groups=mesh['wide'=16,'narrow'=8] {'wide','narrow'}, dimensions={0} | all-to-all | bytes 2949120 | tf_op jit(solution)/shard_map/all_to_all | solution.py:9
  63.9 14.5 %reshape.48 = bf16[6144,2,60]{2,1,0:T(2,128)(2,1)} reshape(bf16[128,2,2880]{2,1,0:T(2,128)(2,1)} %all_to_all.36) | data formatting | bytes 2949120
  78.4 4.8 %copy.55 = bf16[2,60,128,48]{1,2,3,0:T(8,128)(2,1)} copy(bf16[2,60,128,48]{1,0,3,2:T(2,128)(2,1)} %bitcast.66) | data formatting | bytes 2949120 | tf_op jit(solution)/shard_map/all_to_all | solution.py:9
  83.2 6.9 %all_to_all.33 = bf16[2,7680,48]{1,2,0:T(8,128)(2,1)} reshape(bf16[2,128,60,48]{2,1,3,0:T(8,128)(2,1)} %bitcast.67) | data formatting | bytes 2949120 | tf_op jit(solution)/shard_map/all_to_all | solution.py:9
  90.1 0.0 all-gather.5.cloned.1.call-update
  90.1 0.2 all-gather.3.cloned.1.call-start
  90.4 1.5 copy.38
  91.9 5.0 %reshape.33 = bf16[2,60,8,16,48]{4,3,2,0,1:T(8,128)(2,1)} reshape(bf16[2,60,6144]{2,0,1:T(2,128)(2,1)S(1)} %copy.38) | data formatting | bytes 2949120 | tf_op jit(solution)/shard_map/reshape | solution.py:44
  96.9 10.7 %copy.46 = bf16[2,60,16,8,48]{1,0,4,3,2:T(2,128)(2,1)S(1)} copy(bf16[2,60,16,8,48]{4,2,3,0,1:T(8,128)(2,1)} %bitcast.64) | data formatting | bytes 2949120 | tf_op jit(solution)/shard_map/reshape | solution.py:45
  107.6 6.5 %reshape.45 = bf16[128,2,2880]{2,1,0:T(2,128)(2,1)} reshape(bf16[6144,2,60]{2,1,0:T(2,128)(2,1)S(1)} %bitcast.65) | data formatting | bytes 2949120
  114.1 29.9 %all_to_all.37 = bf16[128,2,2880]{2,1,0:T(2,128)(2,1)} all-to-all(bf16[128,2,2880]{2,1,0:T(2,128)(2,1)} %reshape.45), channel_id=1, replica_groups=mesh['wide'=16,'narrow'=8] {'wide','narrow'}, dimensions={0} | all-to-all | bytes 2949120 | tf_op jit(solution)/shard_map/all_to_all | solution.py:10
  144.0 13.8 %reshape.46 = bf16[6144,2,60]{2,1,0:T(2,128)(2,1)S(1)} reshape(bf16[128,2,2880]{2,1,0:T(2,128)(2,1)} %all_to_all.37) | data formatting | bytes 2949120
  157.8 2.9 copy.56
  160.6 0.0 copy-start.2
  160.6 0.0 copy-start.3
  160.6 0.0 copy-start.4
  160.6 0.0 copy-start.5
  160.6 6.9 %all_to_all.29 = bf16[2,7680,48]{1,2,0:T(8,128)(2,1)} reshape(bf16[2,128,60,48]{2,1,3,0:T(8,128)(2,1)} %bitcast.69) | data formatting | bytes 2949120 | tf_op jit(solution)/shard_map/all_to_all | solution.py:10
  167.6 0.0 all-gather.3.cloned.1.call-update
  167.6 0.0 copy-done.2
  167.6 0.0 copy-done.3
  167.6 0.0 copy-done.4
  167.6 0.0 copy-done.5
  167.7 0.3 select_reduce_fusion
  168.0 0.0 all-gather.5.cloned.1.call-done
  168.0 147.5 %all-gather.3.cloned.1.call-done = bf16[2,7680,768]{1,2,0:T(8,128)(2,1)} async-done(((bf16[2,7680,48]{1,2,0:T(8,128)(2,1)}), bf16[2,7680,768]{1,2,0:T(8,128)(2,1)}) %all-gather.3.cloned.1.call-update) | async-done | bytes 23592976 | tf_op jit(solution)/shard_map/all_gather | solution.py:48
  315.5 0.0 copy-start.6
  315.5 12.3 %fusion = f32[768,384]{1,0:T(8,128)S(1)} fusion(bf16[2,7680,768]{1,2,0:T(8,128)(2,1)} %all-gather.3.cloned.1.call-done, bf16[2,7680,384]{1,2,0:T(8,128)(2,1)} %all-gather.5.cloned.1.call-done), kind=kOutput, calls=%fused_computation.2 | convolution fusion | flops 4529848320 | bytes 18874368 | tf_op jit(solution)/shard_map/gk,gb->kb/dot_general | solution.py:20
  327.9 0.0 copy-done.6
  327.9 9.2 %fusion.4 = f32[1,768,384]{2,1,0:T(8,128)S(1)} fusion(f32[768,384]{1,0:T(8,128)S(1)} %fusion, bf16[2,7680,384]{1,2,0:T(8,128)(2,1)S(1)} %copy-done.6, bf16[2,7680,768]{1,2,0:T(8,128)(2,1)} %all-gather.3.cloned.1.call-done), kind=kOutput, calls=%fused_computation.13 | convolution fusion | flops 4530438144 | bytes 20054016 | tf_op jit(solution)/shard_map/gk,gb->kb/dot_general | solution.py:17
  337.1 0.0 copy-start.1
  337.1 19.4 %fusion.7 = f32[1,768,384]{2,1,0:T(8,128)S(1)} fusion(bf16[2,7680,768]{1,2,0:T(8,128)(2,1)} %all-gather.3.cloned.1.call-done, bf16[2,7680,384]{1,2,0:T(8,128)(2,1)} %all-gather.5.cloned.1.call-done, f32[768]{0:T(1024)S(1)} %sub.10, s32[384]{0:T(512)S(1)} %iota_add_fusion.1, s32[768]{0:T(1024)S(1)} %iota_add_fusion), kind=kOutput, calls=%fused_computation.17 | convolution fusion | flops 9060876288 | bytes 36576768 | tf_op jit(solution)/shard_map/pgk,pgb->kb/dot_general | solution.py:16
  356.5 1.6 pad_maximum_fusion
  358.0 0.0 copy-done.1
  (4 shorter events, 0.0 us)
Async XLA Ops:
  6.5 0.8 copy-start
  6.5 161.5 %all-gather.5.cloned.1.call-start = ((), (), s32[]{:S(2)}) async-start(), calls=%async_computation.3 | async-start | bytes 13271040 | tf_op jit(solution)/shard_map/all_gather | solution.py:47
  90.1 225.4 %all-gather.3.cloned.1.call-start = ((), (), s32[]{:S(2)}) async-start(), calls=%async_computation.2 | async-start | bytes 25067520 | tf_op jit(solution)/shard_map/all_gather | solution.py:48
  160.6 7.0 %copy-start.2 = (s32[768]{0:T(1024)S(1)}, s32[768]{0:T(1024)}, u32[]{:S(2)}) copy-start(s32[768]{0:T(1024)} %param.12) | copy-start | bytes 9220
  160.6 7.0 %copy-start.3 = (s32[768]{0:T(1024)S(1)}, s32[768]{0:T(1024)}, u32[]{:S(2)}) copy-start(s32[768]{0:T(1024)} %param.13) | copy-start | bytes 9220
  160.6 7.0 %copy-start.4 = (f32[300]{0:T(512)S(1)}, f32[300]{0:T(512)}, u32[]{:S(2)}) copy-start(f32[300]{0:T(512)} %param.10) | copy-start | bytes 3604
  160.6 7.0 %copy-start.5 = (f32[300]{0:T(512)S(1)}, f32[300]{0:T(512)}, u32[]{:S(2)}) copy-start(f32[300]{0:T(512)} %param.11) | copy-start | bytes 3604
  315.5 12.4 %copy-start.6 = (bf16[2,7680,384]{1,2,0:T(8,128)(2,1)S(1)}, bf16[2,7680,384]{1,2,0:T(8,128)(2,1)}, u32[]{:S(2)}) copy-start(bf16[2,7680,384]{1,2,0:T(8,128)(2,1)} %all-gather.5.cloned.1.call-done) | copy-start | bytes 35389444
  337.1 21.0 %copy-start.1 = (f32[15360]{0:T(1024)S(1)}, f32[15360]{0:T(1024)}, u32[]{:S(2)}) copy-start(f32[15360]{0:T(1024)} %param.9) | copy-start | bytes 184324
Sparse Core Ops, SparseCore 0:
  90.2 76.9 all-gather.4
  169.3 146.1 all-gather.2
where the time goes:
time: 366 us; the launch traced here: 365 us
  waiting for transfers between devices  148 us (40%)
  local copies, waits for them, and re-layouts  92.2 us (25%)
  blocking collectives  65.3 us (18%)
  matrix products  40.9 us (11%)
  between operations  13.6 us (4%)
  other arithmetic  5.15 us (1%)
    all_gather x1, waiting for transfers between devices, per_device(): lax.all_gather(row_part, 'wide', axis=2, tiled=True)  148 us
    unnamed x18, local copies, waits for them, and re-layouts  47.5 us
    all_to_all x1, blocking collectives, regroup(): lax.all_to_all(first_src, ('wide', 'narrow'), split_axis=2, concat_axis=1...  35.4 us
    all_to_all x1, blocking collectives, regroup(): lax.all_to_all(second_src, ('wide', 'narrow'), split_axis=2, concat_axis=...  29.9 us
    dot_general x1, matrix products, tile_pair(): jnp.einsum('pgk,pgb->kb', row_side, col_side, preferred_element_type=jnp....  19.4 us
    dot_general x1, matrix products, tile_pair(): jnp.einsum('gk,gb->kb', row_side[1], col_side[0], preferred_element_type=...  12.3 us
    all_to_all x2, local copies, waits for them, and re-layouts, regroup(): lax.all_to_all(first_src, ('wide', 'narrow'), split_axis=2, concat_axis=1...  11.7 us
    reshape x1, local copies, waits for them, and re-layouts, per_device(): row_order.transpose(0, 1, 3, 2, 4).reshape(2, local_g, total_trans)  10.7 us
  transfers between devices with their start and end apart: 2, of which 1 were waited for; matrix products, arithmetic and copies ran while one was open for 11% of the time, Pallas kernels for 0%

commit v1 on v0

v1 whole, which is shorter than its diff:
```python
import functools

import jax
import jax.numpy as jnp
from jax import lax
from jax.experimental import pallas as pl
from jax.experimental.pallas import tpu as pltpu
from jax.sharding import PartitionSpec as P

AXES = ("wide", "narrow")
SIDE = 4
BLOCK = 384
ROW_CHUNKS = ((0, 1),)
COL_CHUNKS = ((2, 1, 3, 0),)


def moved(value, dx=0, dy=0, dz=0, core=0, per_core_z=None):
    pairs = []
    for x in range(SIDE):
        for z in range(SIDE):
            for y in range(SIDE):
                for c in range(2):
                    step = dz if per_core_z is None else per_core_z[c]
                    to = ((x + dx) % SIDE, (z + step) % SIDE, (y + dy) % SIDE, (c + core) % 2)
                    pairs.append(
                        (((x * SIDE + z) * SIDE + y) * 2 + c, ((to[0] * SIDE + to[1]) * SIDE + to[2]) * 2 + to[3])
                    )
    return lax.ppermute(value, AXES, pairs)


def prepare_kernel(pos, own, sib, weight, *outs):
    x, y, z, c = pos[0], pos[1], pos[2], pos[3]
    first = c == 0

    def piece(index):
        cut = pl.ds(pl.multiple_of(index * BLOCK, BLOCK), BLOCK)
        mine = own[:, :, cut].astype(jnp.float32)
        other = sib[:, :, cut].astype(jnp.float32)
        zero = jnp.where(first, mine, other)
        one = jnp.where(first, other, mine)
        rows = jnp.concatenate([zero[0], one[0], zero[1], one[1]], axis=0)
        scale = jnp.concatenate([weight[...]] * (BLOCK // 128), axis=1)
        return (rows * scale).astype(jnp.bfloat16)

    at = 0
    for chunk in ROW_CHUNKS:
        for d in range(SIDE):
            for n, i in enumerate(chunk):
                outs[at][n] = piece((2 * lax.rem(y + d, SIDE) + c) * 2 + i)
            at += 1
    for chunk in COL_CHUNKS:
        for part in range(2):
            for n, delta in enumerate(chunk):
                step = 1 + 2 * c if part == 0 else 2 * c
                outs[at][n] = piece(lax.rem(x + delta, SIDE) * SIDE + lax.rem(z + step, SIDE))
            at += 1


def prepare(pos, own, sib, weight):
    rows = own.shape[1] * 4
    shapes = [
        jax.ShapeDtypeStruct((len(chunk), rows, BLOCK), jnp.bfloat16) for chunk in ROW_CHUNKS for _ in range(SIDE)
    ] + [jax.ShapeDtypeStruct((len(chunk), rows, BLOCK), jnp.bfloat16) for chunk in COL_CHUNKS for _ in range(2)]
    vmem = pl.BlockSpec(memory_space=pltpu.VMEM)
    return pl.pallas_call(
        prepare_kernel,
        out_shape=shapes,
        in_specs=[pl.BlockSpec(memory_space=pltpu.SMEM), vmem, vmem, vmem],
        out_specs=[vmem] * len(shapes),
        compiler_params=pltpu.CompilerParams(vmem_limit_bytes=48 * 2**20),
        cost_estimate=pl.CostEstimate(flops=10**6, bytes_accessed=6 * 10**6, transcendentals=0),
        name="prepare",
    )(pos, own, sib, weight)


def tile_kernel(row_parts, col_parts, row_n, col_at, out_dtype, depth, pos, *refs):
    n_row, n_col = len(row_parts), len(col_parts)
    row_refs, col_refs = refs[:n_row], refs[n_row : n_row + n_col]
    out, rbuf, cbuf, sem = refs[n_row + n_col :]
    c = pos[3]
    copies = []
    for ref, places in zip(row_refs, row_parts):
        for index, zpos, ypos in places:
            zat = jnp.where(c == 0, zpos, SIDE - 1 - zpos)
            start = pl.multiple_of((zat * SIDE + ypos) * depth, depth)
            for i in range(row_n):
                copies.append(
                    pltpu.make_async_copy(
                        ref.at[index, i], rbuf.at[pl.ds(start, depth), pl.ds(i * BLOCK, BLOCK)], sem.at[0]
                    )
                )
    for ref, places in zip(col_refs, col_parts):
        for index, zpos, ypos in places:
            start = (zpos * SIDE + ypos) * depth
            copies.append(
                pltpu.make_async_copy(
                    ref.at[index, col_at], cbuf.at[pl.ds(start, depth), pl.ds(0, BLOCK)], sem.at[0]
                )
            )
    for copy in copies:
        copy.start()
    for copy in copies:
        copy.wait()

    def swap(k, carry):
        at = pl.ds(pl.multiple_of(k * depth, depth), depth)
        value = cbuf[at, :BLOCK].astype(jnp.float32)
        turned = jnp.concatenate([value[depth // 2 :], -value[: depth // 2]], axis=0)
        cbuf[at, BLOCK:] = turned.astype(jnp.bfloat16)
        return carry

    lax.fori_loop(0, SIDE * SIDE, swap, 0)
    total = SIDE * SIDE * depth
    for i in range(row_n):
        prod = lax.dot_general(
            rbuf[:, i * BLOCK : (i + 1) * BLOCK],
            cbuf[...],
            (((0,), (0,)), ((), ())),
            preferred_element_type=jnp.float32,
        )
        prod = 2.0 * prod
        out[0, i * BLOCK : (i + 1) * BLOCK, :] = prod[:, :BLOCK].astype(out_dtype)
        out[1, i * BLOCK : (i + 1) * BLOCK, :] = prod[:, BLOCK:].astype(out_dtype)


def tile(pos, row_ops, col_ops, row_n, col_at, out_dtype):
    depth = row_ops[0][0].shape[-2]
    total = depth * SIDE * SIDE
    kernel = functools.partial(
        tile_kernel, [p for _, p in row_ops], [p for _, p in col_ops], row_n, col_at, out_dtype, depth
    )
    n_in = len(row_ops) + len(col_ops)
    return pl.pallas_call(
        kernel,
        out_shape=jax.ShapeDtypeStruct((2, row_n * BLOCK, BLOCK), out_dtype),
        in_specs=[pl.BlockSpec(memory_space=pltpu.SMEM)] + [pl.BlockSpec(memory_space=pl.ANY)] * n_in,
        out_specs=pl.BlockSpec(memory_space=pltpu.VMEM),
        scratch_shapes=[
            pltpu.VMEM((total, row_n * BLOCK), jnp.bfloat16),
            pltpu.VMEM((total, 2 * BLOCK), jnp.bfloat16),
            pltpu.SemaphoreType.DMA((1,)),
        ],
        compiler_params=pltpu.CompilerParams(vmem_limit_bytes=56 * 2**20),
        cost_estimate=pl.CostEstimate(
            flops=4 * total * row_n * BLOCK * BLOCK, bytes_accessed=2 * total * BLOCK * (row_n + 1), transcendentals=0
        ),
        name="tile",
    )(pos, *[a for a, _ in row_ops], *[a for a, _ in col_ops])


def band_lookup(band_ids, table):
    levels = jnp.arange(table.shape[0], dtype=jnp.int32)
    onehot_mask = band_ids[:, None] == levels[None, :]
    return jnp.sum(jnp.where(onehot_mask, table[None, :], 0.0), axis=1)


def per_device(
    pair_density, g_index, coulomb_table, eps_valence, eps_conduction, valence_band, conduction_band
):
    wide_pos, narrow_pos = lax.axis_index("wide"), lax.axis_index("narrow")
    x, z = wide_pos // SIDE, wide_pos % SIDE
    y, c = narrow_pos // 2, narrow_pos % 2
    pos = jnp.stack([x, y, z, c]).astype(jnp.int32)

    sib = moved(pair_density, core=1)
    sib_index = moved(g_index, core=1)
    chip_index = jnp.where(c == 0, jnp.stack([g_index, sib_index]), jnp.stack([sib_index, g_index]))
    weight = jnp.sqrt(jnp.take(coulomb_table, chip_index.reshape(-1)))
    weight = jnp.broadcast_to(jnp.concatenate([weight, weight])[:, None], (4 * g_index.shape[0], 128))
    pieces = prepare(pos, pair_density, sib, weight)
    row_pieces = [pieces[SIDE * n : SIDE * (n + 1)] for n in range(len(ROW_CHUNKS))]
    rest = pieces[SIDE * len(ROW_CHUNKS) :]
    col_pieces = [rest[2 * n : 2 * (n + 1)] for n in range(len(COL_CHUNKS))]

    row_ops = []
    for group in row_pieces:
        mine = jnp.stack([group[0], moved(group[1], dy=1), moved(group[3], dy=-1), moved(group[2], dy=2)])
        below = moved(mine, dz=1)
        above = moved(mine, dz=-1)
        far_a = moved(below[:2], dz=1)
        far_b = moved(above[2:], dz=-1)
        row_ops.append(
            [
                (mine, [(k, 0, k) for k in range(4)]),
                (below, [(k, 1, k) for k in range(4)]),
                (above, [(k, 2, k) for k in range(4)]),
                (far_a, [(k, 3, k) for k in range(2)]),
                (far_b, [(k, 3, k + 2) for k in range(2)]),
            ]
        )
    col_ops = []
    for part0, part1 in col_pieces:
        mine = jnp.stack([moved(part0, per_core_z=(1, -1)), moved(part1, per_core_z=(0, 2))])
        below = moved(mine, dy=1)
        above = moved(mine, dy=-1)
        far_a = moved(below[:1], dy=1)
        far_b = moved(above[1:], dy=-1)
        held = [
            (mine, [(0, 1, 0), (1, 0, 0)]),
            (below, [(0, 1, 1), (1, 0, 1)]),
            (above, [(0, 1, 2), (1, 0, 2)]),
            (far_a, [(0, 1, 3)]),
            (far_b, [(0, 0, 3)]),
        ]
        other = [(moved(a, core=1), [(k, SIDE - 1 - zp, yp) for k, zp, yp in places]) for a, places in held]
        col_ops.append(held + other)

    sums = []
    for rows, chunk in zip(row_ops, ROW_CHUNKS):
        got = {}
        for cols, deltas in zip(col_ops, COL_CHUNKS):
            for n, delta in enumerate(deltas):
                part = tile(pos, rows, cols, len(chunk), n, jnp.float32 if delta == 0 else jnp.bfloat16)
                got[delta] = part if delta == 0 else moved(part, dx=delta)
        sums.append(sum(got[d].astype(jnp.float32) for d in range(1, SIDE)) + got[0])
    total = jnp.concatenate(sums, axis=1)

    row_width, col_width = total.shape[1], total.shape[2]
    row_ids = narrow_pos * row_width + jnp.arange(row_width, dtype=jnp.int32)
    col_ids = wide_pos * col_width + jnp.arange(col_width, dtype=jnp.int32)
    gap = band_lookup(conduction_band, eps_conduction) - band_lookup(valence_band, eps_valence)
    diagonal = jnp.where(row_ids[:, None] == col_ids[None, :], gap[:, None], 0.0)
    return jnp.stack([total[0] + diagonal, total[1]])


def solution(mesh):
    placed = (
        P(None, ("wide", "narrow"), None),
        P(("wide", "narrow")),
        P(),
        P(),
        P(),
        P("narrow"),
        P("narrow"),
    )
    return jax.shard_map(
        per_device, mesh=mesh, in_specs=placed, out_specs=P(None, "narrow", "wide"), check_vma=False
    )
```

time: 366 us -> 186 us (0.51)
  local copies, waits for them, and re-layouts: 92.2 us -> 8.85 us
  blocking collectives: 65.3 us -> 0 us
  waiting for transfers between devices: 148 us -> 94.7 us
  Pallas kernels: 0 us -> 44.1 us
  matrix products: 40.9 us -> 0 us
  starting transfers between devices: 0.22 us -> 33.1 us
  between operations: 13.6 us -> 0.37 us
    all_gather x2 -> x0, waiting for transfers between devices: 148 us -> none  [the longest x1 148 us: per_device(): lax.all_gather(row_part, 'wide', axis=2, tiled=True)]
    ppermute x0 -> x23, waiting for transfers between devices: none -> 94.7 us  [moved(): return lax.ppermute(value, AXES, pairs)]
    all_to_all x2 -> x0, blocking collectives: 65.3 us -> none  [the longest x1 35.4 us: regroup(): lax.all_to_all(first_src, ('wide', 'narrow'), split_axis=2, concat_axis=1...]
    pallas_call x0 -> x5, Pallas kernels: none -> 44.1 us  [the longest x4 42.4 us: tile(): pl.pallas_call(kernel, out_shape=jax.ShapeDtypeStruct((2, row_n * BLOCK,...]
    dot_general x3 -> x0, matrix products: 40.9 us -> none  [the longest x1 19.4 us: tile_pair(): jnp.einsum('pgk,pgb->kb', row_side, col_side, preferred_element_type=jnp....]
    unnamed x18 -> x49, local copies, waits for them, and re-layouts: 47.5 us -> 6.7 us
    ppermute x0 -> x23, starting transfers between devices: none -> 33.1 us  [moved(): return lax.ppermute(value, AXES, pairs)]
    all_to_all x4 -> x0, local copies, waits for them, and re-layouts: 21.5 us -> none  [the longest x2 11.7 us: regroup(): lax.all_to_all(first_src, ('wide', 'narrow'), split_axis=2, concat_axis=1...]
  transfers between devices with their start and end apart: 2 -> 23, of which waited for: 1 -> 11; matrix products, arithmetic and copies ran while one was open for 11% -> 2% of each run, Pallas kernels for 0% -> 17%
where the time goes in v1:
time: 186 us; the launch traced here: 185 us
  waiting for transfers between devices  94.7 us (51%)
  Pallas kernels  44.1 us (24%)
  starting transfers between devices  33.1 us (18%)
  local copies, waits for them, and re-layouts  8.85 us (5%)
  other arithmetic  3.83 us (2%)
    ppermute x23, waiting for transfers between devices, moved(): return lax.ppermute(value, AXES, pairs)  94.7 us
    pallas_call x4, Pallas kernels, tile(): pl.pallas_call(kernel, out_shape=jax.ShapeDtypeStruct((2, row_n * BLOCK,...  42.4 us
    ppermute x23, starting transfers between devices, moved(): return lax.ppermute(value, AXES, pairs)  33.1 us
    unnamed x49, local copies, waits for them, and re-layouts  6.7 us
  transfers between devices with their start and end apart: 23, of which 11 were waited for; matrix products, arithmetic and copies ran while one was open for 2% of the time, Pallas kernels for 17%

profile of v1, /device:TPU:1, one launch (start us, length us, event | category | flops | bytes accessed | tf_op | source)
XLA Modules:
  0.0 184.9 jit_solution(18089461166822498580)
XLA Ops:
  0.0 1.4 collective-permute-start
  1.4 0.1 pad_add_fusion.pos
  1.5 1.8 copy.14.own
  3.4 1.2 collective-permute-done.1
  4.5 0.1 select_n.88
  4.6 0.1 select_n.86
  4.7 1.1 gather_fusion
  5.9 0.1 pad_maximum_fusion.3
  6.0 0.5 copy.15.sib
  6.4 0.1 broadcast_in_dim.52.weight
  6.5 1.6 prepare.1
  8.2 3.9 %collective-permute-start.9 = (bf16[4,240,384]{2,1,0:T(8,128)(2,1)S(1)}, bf16[4,240,384]{2,1,0:T(8,128)(2,1)S(1)}, u32[]{:S(2)}, u32[]{:S(2)}) collective-permute-start(bf16[4,240,384]{2,1,0:T(8,128)(2,1)S(1)} %get-tuple-element.15), channel_id=1, source_target_pairs={{0,8},{1,25},{2,10},{3,27},{4,12},{5,29},{6,14},{7,31},{8,16},{9,1... | collective-permute-start | bytes 2211848 | tf_op jit(solution)/shard_map/ppermute | solution.py:28
  12.1 1.9 %collective-permute-start.10 = (bf16[4,240,384]{2,1,0:T(8,128)(2,1)S(1)}, bf16[4,240,384]{2,1,0:T(8,128)(2,1)S(1)}, u32[]{:S(2)}, u32[]{:S(2)}) collective-permute-start(bf16[4,240,384]{2,1,0:T(8,128)(2,1)S(1)} %get-tuple-element.16), channel_id=1, source_target_pairs={{0,0},{1,17},{2,2},{3,19},{4,4},{5,21},{6,6},{7,23},{8,8},{9,25},{... | collective-permute-start | bytes 2211848 | tf_op jit(solution)/shard_map/ppermute | solution.py:28
  14.0 3.0 %collective-permute-start.4 = (bf16[2,240,384]{2,1,0:T(8,128)(2,1)S(1)}, bf16[2,240,384]{2,1,0:T(8,128)(2,1)S(1)}, u32[]{:S(2)}, u32[]{:S(2)}) collective-permute-start(bf16[2,240,384]{2,1,0:T(8,128)(2,1)S(1)} %get-tuple-element.14), channel_id=1, source_target_pairs={{0,4},{1,5},{2,6},{3,7},{4,0},{5,1},{6,2},{7,3},{8,12},{9,13},{10,... | collective-permute-start | bytes 1105928 | tf_op jit(solution)/shard_map/ppermute | solution.py:28
  17.0 0.4 collective-permute-start.2
  17.4 2.3 %collective-permute-start.3 = (bf16[2,240,384]{2,1,0:T(8,128)(2,1)S(1)}, bf16[2,240,384]{2,1,0:T(8,128)(2,1)S(1)}, u32[]{:S(2)}, u32[]{:S(2)}) collective-permute-start(bf16[2,240,384]{2,1,0:T(8,128)(2,1)S(1)} %get-tuple-element.13), channel_id=1, source_target_pairs={{0,6},{1,7},{2,0},{3,1},{4,2},{5,3},{6,4},{7,5},{8,14},{9,15},{10,... | collective-permute-start | bytes 1105928 | tf_op jit(solution)/shard_map/ppermute | solution.py:28
  19.7 6.3 %collective-permute-done.4 = bf16[2,240,384]{2,1,0:T(8,128)(2,1)S(1)} collective-permute-done((bf16[2,240,384]{2,1,0:T(8,128)(2,1)S(1)}, bf16[2,240,384]{2,1,0:T(8,128)(2,1)S(1)}, u32[]{:S(2)}, u32[]{:S(2)}) %collective-permute-start.4) | collective-permute-done | bytes 368672 | tf_op jit(solution)/shard_map/ppermute | solution.py:28
  26.0 5.8 %collective-permute-done.2 = bf16[2,240,384]{2,1,0:T(8,128)(2,1)S(1)} collective-permute-done((bf16[2,240,384]{2,1,0:T(8,128)(2,1)S(1)}, bf16[2,240,384]{2,1,0:T(8,128)(2,1)S(1)}, u32[]{:S(2)}, u32[]{:S(2)}) %collective-permute-start.2) | collective-permute-done | bytes 368672 | tf_op jit(solution)/shard_map/ppermute | solution.py:28
  31.8 0.2 collective-permute-done.3
  32.0 0.2 pad_maximum_fusion.1.refs_0_
  32.2 1.7 collective-permute-start.5
  33.9 0.2 pad_maximum_fusion.2.refs_5_
  34.1 1.2 collective-permute-start.11
  35.3 1.6 collective-permute-start.12
  36.9 1.0 collective-permute-start.6
  37.9 1.3 collective-permute-start.15
  39.2 27.9 %collective-permute-done.5.refs_1_ = bf16[4,2,240,384]{3,2,1,0:T(8,128)(2,1)S(1)} collective-permute-done((bf16[4,2,240,384]{3,2,1,0:T(8,128)(2,1)S(1)}, bf16[4,2,240,384]{3,2,1,0:T(8,128)(2,1)S(1)}, u32[]{:S(2)}, u32[]{:S(2)}) %collective-permute-start.5) | collective-permute-done | bytes 1474592 | tf_op jit(solution)/shard_map/ppermute | solution.py:28
  67.2 0.1 slice.26
  67.3 0.5 collective-permute-start.7
  67.8 1.0 collective-permute-done.11.refs_6_
  68.8 0.1 slice.28
  68.9 0.4 collective-permute-start.13
  69.3 0.1 slice.29
  69.3 2.4 %collective-permute-start.14 = (bf16[1,4,240,384]{3,2,1,0:T(8,128)(2,1)S(1)}, bf16[1,4,240,384]{3,2,1,0:T(8,128)(2,1)S(1)}, u32[]{:S(2)}, u32[]{:S(2)}) collective-permute-start(bf16[1,4,240,384]{3,2,1,0:T(8,128)(2,1)S(1)} %slice.29), channel_id=1, source_target_pairs={{0,6},{1,7},{2,0},{3,1},{4,2},{5,3},{6,4},{7,5},{8,14},{9,15},{10,... | collective-permute-start | bytes 2211848 | tf_op jit(solution)/shard_map/ppermute | solution.py:28
  71.8 2.0 %collective-permute-start.16 = (bf16[2,4,240,384]{3,2,1,0:T(8,128)(2,1)S(1)}, bf16[2,4,240,384]{3,2,1,0:T(8,128)(2,1)S(1)}, u32[]{:S(2)}, u32[]{:S(2)}) collective-permute-start(bf16[2,4,240,384]{3,2,1,0:T(8,128)(2,1)S(1)} %collective-permute-done.11.refs_6_), channel_id=1, source_target_pairs={{0,1},{1,0},{2,3},{3,2},{4,5},{5,4},{6,7},{7,6},{8,9},{9,8},{10,11... | collective-permute-start | bytes 4423688 | tf_op jit(solution)/shard_map/ppermute | solution.py:28
  73.8 0.1 collective-permute-start.17
  73.9 0.1 slice.27
  74.0 11.6 %collective-permute-done.7.refs_3_ = bf16[2,2,240,384]{3,2,1,0:T(8,128)(2,1)S(1)} collective-permute-done((bf16[2,2,240,384]{3,2,1,0:T(8,128)(2,1)S(1)}, bf16[2,2,240,384]{3,2,1,0:T(8,128)(2,1)S(1)}, u32[]{:S(2)}, u32[]{:S(2)}) %collective-permute-start.7) | collective-permute-done | bytes 737312 | tf_op jit(solution)/shard_map/ppermute | solution.py:28
  85.5 0.2 collective-permute-start.8
  85.7 1.1 collective-permute-done.13.refs_8_
  86.8 2.3 %collective-permute-start.18 = (bf16[1,4,240,384]{3,2,1,0:T(8,128)(2,1)S(1)}, bf16[1,4,240,384]{3,2,1,0:T(8,128)(2,1)S(1)}, u32[]{:S(2)}, u32[]{:S(2)}) collective-permute-start(bf16[1,4,240,384]{3,2,1,0:T(8,128)(2,1)S(1)} %collective-permute-done.13.refs_8_), channel_id=1, source_target_pairs={{0,1},{1,0},{2,3},{3,2},{4,5},{5,4},{6,7},{7,6},{8,9},{9,8},{10,11... | collective-permute-start | bytes 2211848 | tf_op jit(solution)/shard_map/ppermute | solution.py:28
  89.1 0.3 collective-permute-start.19
  89.3 12.2 %collective-permute-done.8.refs_4_ = bf16[2,2,240,384]{3,2,1,0:T(8,128)(2,1)S(1)} collective-permute-done((bf16[2,2,240,384]{3,2,1,0:T(8,128)(2,1)S(1)}, bf16[2,2,240,384]{3,2,1,0:T(8,128)(2,1)S(1)}, u32[]{:S(2)}, u32[]{:S(2)}) %collective-permute-start.8) | collective-permute-done | bytes 737312 | tf_op jit(solution)/shard_map/ppermute | solution.py:28
  101.6 0.8 copy-done.15
  102.5 0.3 copy-done.16
  102.8 0.2 copy-done.14
  103.0 0.9 copy-done.9
  103.9 1.1 copy-done.10
  105.0 10.5 %tile.4 = bf16[2,768,384]{2,1,0:T(8,128)(2,1)} custom-call(s32[4]{0:T(128)} %copy-done.1, bf16[4,2,240,384]{3,2,1,0:T(8,128)(2,1)} %copy-done.2, bf16[4,2,240,384]{3,2,1,0:T(8,128)(2,1)} %copy-done.4, bf16[4,2,240,384]{3,2,1,0:T(8,128)(2,1)} %copy-done.7, bf16[2,2,240,384]{3,2,1,0:T(8,128)(2,1)} %copy-done.11, bf16[2,2,240,384]{3,2,1,0:T(8,128)(2,1)} %copy-done.14, ...), custom_call_target="tpu_custom_call" | custom-call | flops 4529848320 | bytes 8847360 | tf_op jit(solution)/shard_map/tile/pallas_call | solution.py:133
  115.5 1.3 collective-permute-start.20
  116.8 10.5 %tile.5 = bf16[2,768,384]{2,1,0:T(8,128)(2,1)} custom-call(s32[4]{0:T(128)} %copy-done.1, bf16[4,2,240,384]{3,2,1,0:T(8,128)(2,1)} %copy-done.2, bf16[4,2,240,384]{3,2,1,0:T(8,128)(2,1)} %copy-done.4, bf16[4,2,240,384]{3,2,1,0:T(8,128)(2,1)} %copy-done.7, bf16[2,2,240,384]{3,2,1,0:T(8,128)(2,1)} %copy-done.11, bf16[2,2,240,384]{3,2,1,0:T(8,128)(2,1)} %copy-done.14, ...), custom_call_target="tpu_custom_call" | custom-call | flops 4529848320 | bytes 8847360 | tf_op jit(solution)/shard_map/tile/pallas_call | solution.py:133
  127.3 0.0 copy-start.17
  127.4 0.0 copy-start.19
  127.4 0.0 copy-start.20
  127.4 2.5 %collective-permute-start.21 = (bf16[2,768,384]{2,1,0:T(8,128)(2,1)}, bf16[2,768,384]{2,1,0:T(8,128)(2,1)S(1)}, u32[]{:S(2)}, u32[]{:S(2)}) collective-permute-start(bf16[2,768,384]{2,1,0:T(8,128)(2,1)} %tile.5), channel_id=1, source_target_pairs={{0,64},{1,65},{2,66},{3,67},{4,68},{5,69},{6,70},{7,71},{8,72},{9,... | collective-permute-start | bytes 3538952 | tf_op jit(solution)/shard_map/ppermute | solution.py:28
  129.9 10.5 %tile.6 = bf16[2,768,384]{2,1,0:T(8,128)(2,1)} custom-call(s32[4]{0:T(128)} %copy-done.1, bf16[4,2,240,384]{3,2,1,0:T(8,128)(2,1)} %copy-done.2, bf16[4,2,240,384]{3,2,1,0:T(8,128)(2,1)} %copy-done.4, bf16[4,2,240,384]{3,2,1,0:T(8,128)(2,1)} %copy-done.7, bf16[2,2,240,384]{3,2,1,0:T(8,128)(2,1)} %copy-done.11, bf16[2,2,240,384]{3,2,1,0:T(8,128)(2,1)} %copy-done.14, ...), custom_call_target="tpu_custom_call" | custom-call | flops 4529848320 | bytes 8847360 | tf_op jit(solution)/shard_map/tile/pallas_call | solution.py:133
  140.4 1.4 collective-permute-start.22
  141.9 0.3 select_reduce_fusion
  142.2 10.9 %tile.7 = f32[2,768,384]{2,1,0:T(8,128)} custom-call(s32[4]{0:T(128)} %copy-done.1, bf16[4,2,240,384]{3,2,1,0:T(8,128)(2,1)} %copy-done.2, bf16[4,2,240,384]{3,2,1,0:T(8,128)(2,1)} %copy-done.4, bf16[4,2,240,384]{3,2,1,0:T(8,128)(2,1)} %copy-done.7, bf16[2,2,240,384]{3,2,1,0:T(8,128)(2,1)} %copy-done.11, bf16[2,2,240,384]{3,2,1,0:T(8,128)(2,1)} %copy-done.14, ...), custom_call_target="tpu_custom_call" | custom-call | flops 4529848320 | bytes 8847360 | tf_op jit(solution)/shard_map/tile/pallas_call | solution.py:133
  153.2 14.7 %collective-permute-done.21 = bf16[2,768,384]{2,1,0:T(8,128)(2,1)S(1)} collective-permute-done((bf16[2,768,384]{2,1,0:T(8,128)(2,1)}, bf16[2,768,384]{2,1,0:T(8,128)(2,1)S(1)}, u32[]{:S(2)}, u32[]{:S(2)}) %collective-permute-start.21) | collective-permute-done | bytes 1179680 | tf_op jit(solution)/shard_map/ppermute | solution.py:28
  167.9 12.6 %collective-permute-done.22 = bf16[2,768,384]{2,1,0:T(8,128)(2,1)} collective-permute-done((bf16[2,768,384]{2,1,0:T(8,128)(2,1)}, bf16[2,768,384]{2,1,0:T(8,128)(2,1)}, u32[]{:S(2)}, u32[]{:S(2)}) %collective-permute-start.22) | collective-permute-done | bytes 1179680 | tf_op jit(solution)/shard_map/ppermute | solution.py:28
  180.5 2.6 %add_add_fusion = f32[2,768,384]{2,1,0:T(8,128)S(1)} fusion(f32[2,768,384]{2,1,0:T(8,128)} %tile.7, bf16[2,768,384]{2,1,0:T(8,128)(2,1)} %collective-permute-done.22, bf16[2,768,384]{2,1,0:T(8,128)(2,1)S(1)} %collective-permute-done.21, bf16[2,768,384]{2,1,0:T(8,128)(2,1)S(1)} %collective-permute-done.20), kind=kLoop, calls=%fused_computation.2 | loop fusion | flops 3538944 | bytes 8257536 | tf_op jit(solution)/shard_map/add | solution.py:215
  183.1 0.3 slice_add_fusion
  183.5 1.4 copy-done.23
  (60 shorter events, 0.2 us)
Async XLA Ops:
  0.0 4.7 %copy-start = (f32[15360]{0:T(1024)S(1)}, f32[15360]{0:T(1024)}, u32[]{:S(2)}) copy-start(f32[15360]{0:T(1024)} %param.9) | copy-start | bytes 184324
  0.0 6.0 %collective-permute-start = (bf16[2,60,6144]{2,0,1:T(2,128)(2,1)}, bf16[2,60,6144]{2,0,1:T(2,128)(2,1)S(1)}, u32[]{:S(2)}, u32[]{:S(2)}) collective-permute-start(bf16[2,60,6144]{2,0,1:T(2,128)(2,1)} %param.7), channel_id=1, source_target_pairs={{0,1},{1,0},{2,3},{3,2},{4,5},{5,4},{6,7},{7,6},{8,9},{9,8},{10,11... | collective-permute-start | bytes 4423688 | tf_op jit(solution)/shard_map/ppermute | solution.py:28
  1.4 3.1 %collective-permute-start.1 = (s32[60]{0:T(128)}, s32[60]{0:T(128)S(1)}, u32[]{:S(2)}, u32[]{:S(2)}) collective-permute-start(s32[60]{0:T(128)} %param.8), channel_id=1, source_target_pairs={{0,1},{1,0},{2,3},{3,2},{4,5},{5,4},{6,7},{7,6},{8,9},{9,8},{10,11... | collective-permute-start | bytes 728 | tf_op jit(solution)/shard_map/ppermute | solution.py:28
  1.5 5.0 %copy-start.1 = (s32[4]{0:T(128)}, s32[4]{0:T(128)S(1)}, u32[]{:S(2)}) copy-start(s32[4]{0:T(128)S(1)} %pad_add_fusion.pos) | copy-start | bytes 52
  1.5 3.0 %copy-start.21 = (s32[60]{0:T(128)S(1)}, s32[60]{0:T(128)}, u32[]{:S(2)}) copy-start(s32[60]{0:T(128)} %param.8) | copy-start | bytes 724
  8.2 25.7 %collective-permute-start.9 = (bf16[4,240,384]{2,1,0:T(8,128)(2,1)S(1)}, bf16[4,240,384]{2,1,0:T(8,128)(2,1)S(1)}, u32[]{:S(2)}, u32[]{:S(2)}) collective-permute-start(bf16[4,240,384]{2,1,0:T(8,128)(2,1)S(1)} %get-tuple-element.15), channel_id=1, source_target_pairs={{0,8},{1,25},{2,10},{3,27},{4,12},{5,29},{6,14},{7,31},{8,16},{9,1... | collective-permute-start | bytes 2211848 | tf_op jit(solution)/shard_map/ppermute | solution.py:28
  12.1 21.8 %collective-permute-start.10 = (bf16[4,240,384]{2,1,0:T(8,128)(2,1)S(1)}, bf16[4,240,384]{2,1,0:T(8,128)(2,1)S(1)}, u32[]{:S(2)}, u32[]{:S(2)}) collective-permute-start(bf16[4,240,384]{2,1,0:T(8,128)(2,1)S(1)} %get-tuple-element.16), channel_id=1, source_target_pairs={{0,0},{1,17},{2,2},{3,19},{4,4},{5,21},{6,6},{7,23},{8,8},{9,25},{... | collective-permute-start | bytes 2211848 | tf_op jit(solution)/shard_map/ppermute | solution.py:28
  14.0 12.0 %collective-permute-start.4 = (bf16[2,240,384]{2,1,0:T(8,128)(2,1)S(1)}, bf16[2,240,384]{2,1,0:T(8,128)(2,1)S(1)}, u32[]{:S(2)}, u32[]{:S(2)}) collective-permute-start(bf16[2,240,384]{2,1,0:T(8,128)(2,1)S(1)} %get-tuple-element.14), channel_id=1, source_target_pairs={{0,4},{1,5},{2,6},{3,7},{4,0},{5,1},{6,2},{7,3},{8,12},{9,13},{10,... | collective-permute-start | bytes 1105928 | tf_op jit(solution)/shard_map/ppermute | solution.py:28
  17.0 14.8 %collective-permute-start.2 = (bf16[2,240,384]{2,1,0:T(8,128)(2,1)S(1)}, bf16[2,240,384]{2,1,0:T(8,128)(2,1)S(1)}, u32[]{:S(2)}, u32[]{:S(2)}) collective-permute-start(bf16[2,240,384]{2,1,0:T(8,128)(2,1)S(1)} %get-tuple-element.12), channel_id=1, source_target_pairs={{0,2},{1,3},{2,4},{3,5},{4,6},{5,7},{6,0},{7,1},{8,10},{9,11},{10,... | collective-permute-start | bytes 1105928 | tf_op jit(solution)/shard_map/ppermute | solution.py:28
  17.4 14.6 %collective-permute-start.3 = (bf16[2,240,384]{2,1,0:T(8,128)(2,1)S(1)}, bf16[2,240,384]{2,1,0:T(8,128)(2,1)S(1)}, u32[]{:S(2)}, u32[]{:S(2)}) collective-permute-start(bf16[2,240,384]{2,1,0:T(8,128)(2,1)S(1)} %get-tuple-element.13), channel_id=1, source_target_pairs={{0,6},{1,7},{2,0},{3,1},{4,2},{5,3},{6,4},{7,5},{8,14},{9,15},{10,... | collective-permute-start | bytes 1105928 | tf_op jit(solution)/shard_map/ppermute | solution.py:28
  32.2 4.7 %copy-start.2 = (bf16[4,2,240,384]{3,2,1,0:T(8,128)(2,1)}, bf16[4,2,240,384]{3,2,1,0:T(8,128)(2,1)S(1)}, u32[]{:S(2)}) copy-start(bf16[4,2,240,384]{3,2,1,0:T(8,128)(2,1)S(1)} %pad_maximum_fusion.1.refs_0_) | copy-start | bytes 4423684
  32.2 35.0 %collective-permute-start.5 = (bf16[4,2,240,384]{3,2,1,0:T(8,128)(2,1)S(1)}, bf16[4,2,240,384]{3,2,1,0:T(8,128)(2,1)S(1)}, u32[]{:S(2)}, u32[]{:S(2)}) collective-permute-start(bf16[4,2,240,384]{3,2,1,0:T(8,128)(2,1)S(1)} %pad_maximum_fusion.1.refs_0_), channel_id=1, source_target_pairs={{0,8},{1,9},{2,10},{3,11},{4,12},{5,13},{6,14},{7,15},{8,16},{9,17... | collective-permute-start | bytes 4423688 | tf_op jit(solution)/shard_map/ppermute | solution.py:28
  34.1 34.7 %copy-start.3 = (bf16[2,4,240,384]{3,2,1,0:T(8,128)(2,1)}, bf16[2,4,240,384]{3,2,1,0:T(8,128)(2,1)S(1)}, u32[]{:S(2)}) copy-start(bf16[2,4,240,384]{3,2,1,0:T(8,128)(2,1)S(1)} %pad_maximum_fusion.2.refs_5_) | copy-start | bytes 4423684
  34.1 34.6 %collective-permute-start.11 = (bf16[2,4,240,384]{3,2,1,0:T(8,128)(2,1)S(1)}, bf16[2,4,240,384]{3,2,1,0:T(8,128)(2,1)S(1)}, u32[]{:S(2)}, u32[]{:S(2)}) collective-permute-start(bf16[2,4,240,384]{3,2,1,0:T(8,128)(2,1)S(1)} %pad_maximum_fusion.2.refs_5_), channel_id=1, source_target_pairs={{0,2},{1,3},{2,4},{3,5},{4,6},{5,7},{6,0},{7,1},{8,10},{9,11},{10,... | collective-permute-start | bytes 4423688 | tf_op jit(solution)/shard_map/ppermute | solution.py:28
  35.3 33.9 %collective-permute-start.12 = (bf16[2,4,240,384]{3,2,1,0:T(8,128)(2,1)S(1)}, bf16[2,4,240,384]{3,2,1,0:T(8,128)(2,1)S(1)}, u32[]{:S(2)}, u32[]{:S(2)}) collective-permute-start(bf16[2,4,240,384]{3,2,1,0:T(8,128)(2,1)S(1)} %pad_maximum_fusion.2.refs_5_), channel_id=1, source_target_pairs={{0,6},{1,7},{2,0},{3,1},{4,2},{5,3},{6,4},{7,5},{8,14},{9,15},{10,... | collective-permute-start | bytes 4423688 | tf_op jit(solution)/shard_map/ppermute | solution.py:28
  36.9 34.9 %collective-permute-start.6 = (bf16[4,2,240,384]{3,2,1,0:T(8,128)(2,1)S(1)}, bf16[4,2,240,384]{3,2,1,0:T(8,128)(2,1)S(1)}, u32[]{:S(2)}, u32[]{:S(2)}) collective-permute-start(bf16[4,2,240,384]{3,2,1,0:T(8,128)(2,1)S(1)} %pad_maximum_fusion.1.refs_0_), channel_id=1, source_target_pairs={{0,24},{1,25},{2,26},{3,27},{4,28},{5,29},{6,30},{7,31},{8,0},{9,1... | collective-permute-start | bytes 4423688 | tf_op jit(solution)/shard_map/ppermute | solution.py:28
  37.9 35.8 %collective-permute-start.15 = (bf16[2,4,240,384]{3,2,1,0:T(8,128)(2,1)S(1)}, bf16[2,4,240,384]{3,2,1,0:T(8,128)(2,1)S(1)}, u32[]{:S(2)}, u32[]{:S(2)}) collective-permute-start(bf16[2,4,240,384]{3,2,1,0:T(8,128)(2,1)S(1)} %pad_maximum_fusion.2.refs_5_), channel_id=1, source_target_pairs={{0,1},{1,0},{2,3},{3,2},{4,5},{5,4},{6,7},{7,6},{8,9},{9,8},{10,11... | collective-permute-start | bytes 4423688 | tf_op jit(solution)/shard_map/ppermute | solution.py:28
  67.2 1.7 copy-start.4
  67.3 18.2 %collective-permute-start.7 = (bf16[2,2,240,384]{3,2,1,0:T(8,128)(2,1)S(1)}, bf16[2,2,240,384]{3,2,1,0:T(8,128)(2,1)S(1)}, u32[]{:S(2)}, u32[]{:S(2)}) collective-permute-start(bf16[2,2,240,384]{3,2,1,0:T(8,128)(2,1)S(1)} %slice.26), channel_id=1, source_target_pairs={{0,8},{1,9},{2,10},{3,11},{4,12},{5,13},{6,14},{7,15},{8,16},{9,17... | collective-permute-start | bytes 2211848 | tf_op jit(solution)/shard_map/ppermute | solution.py:28
  68.8 3.0 %copy-start.5 = (bf16[2,4,240,384]{3,2,1,0:T(8,128)(2,1)}, bf16[2,4,240,384]{3,2,1,0:T(8,128)(2,1)S(1)}, u32[]{:S(2)}) copy-start(bf16[2,4,240,384]{3,2,1,0:T(8,128)(2,1)S(1)} %collective-permute-done.11.refs_6_) | copy-start | bytes 4423684
  68.9 17.9 %collective-permute-start.13 = (bf16[1,4,240,384]{3,2,1,0:T(8,128)(2,1)S(1)}, bf16[1,4,240,384]{3,2,1,0:T(8,128)(2,1)S(1)}, u32[]{:S(2)}, u32[]{:S(2)}) collective-permute-start(bf16[1,4,240,384]{3,2,1,0:T(8,128)(2,1)S(1)} %slice.28), channel_id=1, source_target_pairs={{0,2},{1,3},{2,4},{3,5},{4,6},{5,7},{6,0},{7,1},{8,10},{9,11},{10,... | collective-permute-start | bytes 2211848 | tf_op jit(solution)/shard_map/ppermute | solution.py:28
  69.3 4.7 %copy-start.6 = (bf16[2,4,240,384]{3,2,1,0:T(8,128)(2,1)}, bf16[2,4,240,384]{3,2,1,0:T(8,128)(2,1)S(1)}, u32[]{:S(2)}) copy-start(bf16[2,4,240,384]{3,2,1,0:T(8,128)(2,1)S(1)} %collective-permute-done.12.refs_7_) | copy-start | bytes 4423684
  69.3 19.7 %collective-permute-start.14 = (bf16[1,4,240,384]{3,2,1,0:T(8,128)(2,1)S(1)}, bf16[1,4,240,384]{3,2,1,0:T(8,128)(2,1)S(1)}, u32[]{:S(2)}, u32[]{:S(2)}) collective-permute-start(bf16[1,4,240,384]{3,2,1,0:T(8,128)(2,1)S(1)} %slice.29), channel_id=1, source_target_pairs={{0,6},{1,7},{2,0},{3,1},{4,2},{5,3},{6,4},{7,5},{8,14},{9,15},{10,... | collective-permute-start | bytes 2211848 | tf_op jit(solution)/shard_map/ppermute | solution.py:28
  71.8 29.8 %copy-start.7 = (bf16[4,2,240,384]{3,2,1,0:T(8,128)(2,1)}, bf16[4,2,240,384]{3,2,1,0:T(8,128)(2,1)S(1)}, u32[]{:S(2)}) copy-start(bf16[4,2,240,384]{3,2,1,0:T(8,128)(2,1)S(1)} %collective-permute-done.6.refs_2_) | copy-start | bytes 4423684
  71.8 29.8 %collective-permute-start.16 = (bf16[2,4,240,384]{3,2,1,0:T(8,128)(2,1)S(1)}, bf16[2,4,240,384]{3,2,1,0:T(8,128)(2,1)S(1)}, u32[]{:S(2)}, u32[]{:S(2)}) collective-permute-start(bf16[2,4,240,384]{3,2,1,0:T(8,128)(2,1)S(1)} %collective-permute-done.11.refs_6_), channel_id=1, source_target_pairs={{0,1},{1,0},{2,3},{3,2},{4,5},{5,4},{6,7},{7,6},{8,9},{9,8},{10,11... | collective-permute-start | bytes 4423688 | tf_op jit(solution)/shard_map/ppermute | solution.py:28
  73.8 27.9 %copy-start.8 = (bf16[2,4,240,384]{3,2,1,0:T(8,128)(2,1)}, bf16[2,4,240,384]{3,2,1,0:T(8,128)(2,1)S(1)}, u32[]{:S(2)}) copy-start(bf16[2,4,240,384]{3,2,1,0:T(8,128)(2,1)S(1)} %collective-permute-done.15.refs_10_) | copy-start | bytes 4423684
  73.8 29.0 %collective-permute-start.17 = (bf16[2,4,240,384]{3,2,1,0:T(8,128)(2,1)S(1)}, bf16[2,4,240,384]{3,2,1,0:T(8,128)(2,1)S(1)}, u32[]{:S(2)}, u32[]{:S(2)}) collective-permute-start(bf16[2,4,240,384]{3,2,1,0:T(8,128)(2,1)S(1)} %collective-permute-done.12.refs_7_), channel_id=1, source_target_pairs={{0,1},{1,0},{2,3},{3,2},{4,5},{5,4},{6,7},{7,6},{8,9},{9,8},{10,11... | collective-permute-start | bytes 4423688 | tf_op jit(solution)/shard_map/ppermute | solution.py:28
  85.5 16.1 %copy-start.11 = (bf16[2,2,240,384]{3,2,1,0:T(8,128)(2,1)}, bf16[2,2,240,384]{3,2,1,0:T(8,128)(2,1)S(1)}, u32[]{:S(2)}) copy-start(bf16[2,2,240,384]{3,2,1,0:T(8,128)(2,1)S(1)} %collective-permute-done.7.refs_3_) | copy-start | bytes 2211844
  85.5 16.0 %collective-permute-start.8 = (bf16[2,2,240,384]{3,2,1,0:T(8,128)(2,1)S(1)}, bf16[2,2,240,384]{3,2,1,0:T(8,128)(2,1)S(1)}, u32[]{:S(2)}, u32[]{:S(2)}) collective-permute-start(bf16[2,2,240,384]{3,2,1,0:T(8,128)(2,1)S(1)} %slice.27), channel_id=1, source_target_pairs={{0,24},{1,25},{2,26},{3,27},{4,28},{5,29},{6,30},{7,31},{8,0},{9,1... | collective-permute-start | bytes 2211848 | tf_op jit(solution)/shard_map/ppermute | solution.py:28
  86.8 14.8 %copy-start.12 = (bf16[1,4,240,384]{3,2,1,0:T(8,128)(2,1)}, bf16[1,4,240,384]{3,2,1,0:T(8,128)(2,1)S(1)}, u32[]{:S(2)}) copy-start(bf16[1,4,240,384]{3,2,1,0:T(8,128)(2,1)S(1)} %collective-permute-done.13.refs_8_) | copy-start | bytes 2211844
  86.8 14.8 %collective-permute-start.18 = (bf16[1,4,240,384]{3,2,1,0:T(8,128)(2,1)S(1)}, bf16[1,4,240,384]{3,2,1,0:T(8,128)(2,1)S(1)}, u32[]{:S(2)}, u32[]{:S(2)}) collective-permute-start(bf16[1,4,240,384]{3,2,1,0:T(8,128)(2,1)S(1)} %collective-permute-done.13.refs_8_), channel_id=1, source_target_pairs={{0,1},{1,0},{2,3},{3,2},{4,5},{5,4},{6,7},{7,6},{8,9},{9,8},{10,11... | collective-permute-start | bytes 2211848 | tf_op jit(solution)/shard_map/ppermute | solution.py:28
  89.1 13.7 %copy-start.13 = (bf16[1,4,240,384]{3,2,1,0:T(8,128)(2,1)}, bf16[1,4,240,384]{3,2,1,0:T(8,128)(2,1)S(1)}, u32[]{:S(2)}) copy-start(bf16[1,4,240,384]{3,2,1,0:T(8,128)(2,1)S(1)} %collective-permute-done.14.refs_9_) | copy-start | bytes 2211844
  89.1 12.5 %collective-permute-start.19 = (bf16[1,4,240,384]{3,2,1,0:T(8,128)(2,1)S(1)}, bf16[1,4,240,384]{3,2,1,0:T(8,128)(2,1)S(1)}, u32[]{:S(2)}, u32[]{:S(2)}) collective-permute-start(bf16[1,4,240,384]{3,2,1,0:T(8,128)(2,1)S(1)} %collective-permute-done.14.refs_9_), channel_id=1, source_target_pairs={{0,1},{1,0},{2,3},{3,2},{4,5},{5,4},{6,7},{7,6},{8,9},{9,8},{10,11... | collective-permute-start | bytes 2211848 | tf_op jit(solution)/shard_map/ppermute | solution.py:28
  101.6 1.4 copy-start.14
  101.6 0.9 copy-start.15
  101.6 1.2 copy-start.16
  102.8 1.1 copy-start.9
  103.9 1.1 copy-start.10
  115.5 37.6 %collective-permute-start.20 = (bf16[2,768,384]{2,1,0:T(8,128)(2,1)}, bf16[2,768,384]{2,1,0:T(8,128)(2,1)S(1)}, u32[]{:S(2)}, u32[]{:S(2)}) collective-permute-start(bf16[2,768,384]{2,1,0:T(8,128)(2,1)} %tile.4), channel_id=1, source_target_pairs={{0,32},{1,33},{2,34},{3,35},{4,36},{5,37},{6,38},{7,39},{8,40},{9,... | collective-permute-start | bytes 3538952 | tf_op jit(solution)/shard_map/ppermute | solution.py:28
  127.3 14.5 %copy-start.17 = (s32[768]{0:T(1024)S(1)}, s32[768]{0:T(1024)}, u32[]{:S(2)}) copy-start(s32[768]{0:T(1024)} %param.12) | copy-start | bytes 9220
  127.4 14.5 %copy-start.18 = (s32[768]{0:T(1024)S(1)}, s32[768]{0:T(1024)}, u32[]{:S(2)}) copy-start(s32[768]{0:T(1024)} %param.13) | copy-start | bytes 9220
  127.4 14.5 %copy-start.19 = (f32[300]{0:T(512)S(1)}, f32[300]{0:T(512)}, u32[]{:S(2)}) copy-start(f32[300]{0:T(512)} %param.10) | copy-start | bytes 3604
  127.4 14.5 %copy-start.20 = (f32[300]{0:T(512)S(1)}, f32[300]{0:T(512)}, u32[]{:S(2)}) copy-start(f32[300]{0:T(512)} %param.11) | copy-start | bytes 3604
  127.4 40.5 %collective-permute-start.21 = (bf16[2,768,384]{2,1,0:T(8,128)(2,1)}, bf16[2,768,384]{2,1,0:T(8,128)(2,1)S(1)}, u32[]{:S(2)}, u32[]{:S(2)}) collective-permute-start(bf16[2,768,384]{2,1,0:T(8,128)(2,1)} %tile.5), channel_id=1, source_target_pairs={{0,64},{1,65},{2,66},{3,67},{4,68},{5,69},{6,70},{7,71},{8,72},{9,... | collective-permute-start | bytes 3538952 | tf_op jit(solution)/shard_map/ppermute | solution.py:28
  140.4 40.1 %collective-permute-start.22 = (bf16[2,768,384]{2,1,0:T(8,128)(2,1)}, bf16[2,768,384]{2,1,0:T(8,128)(2,1)}, u32[]{:S(2)}, u32[]{:S(2)}) collective-permute-start(bf16[2,768,384]{2,1,0:T(8,128)(2,1)} %tile.6), channel_id=1, source_target_pairs={{0,96},{1,97},{2,98},{3,99},{4,100},{5,101},{6,102},{7,103},{8,104... | collective-permute-start | bytes 3538952 | tf_op jit(solution)/shard_map/ppermute | solution.py:28
  153.1 30.0 %copy-start.22 = (f32[2,768,384]{2,1,0:T(8,128)S(1)}, f32[2,768,384]{2,1,0:T(8,128)}, u32[]{:S(2)}) copy-start(f32[2,768,384]{2,1,0:T(8,128)} %custom-call.2) | copy-start | bytes 7077892
  183.5 1.4 copy-start.23
